TPU v7x, 128 devices: a whole 4x4x4 slice. The times are simulated.
128 devices in a mesh: cfg: 2 (over x_lo), th: 2 (over core), tw: 4 (over z), hd: 8 (over x_hi, y).
Axes of the slice: x: 4 (x_hi: 2, x_lo: 2; x = x_hi * 2 + x_lo), y: 4, z: 4, core: 2. Of those that a mesh axis runs over, the one named last changes fastest.
Arguments:
- video: bfloat16 [2, 6, 32, 64, 3072], P('cfg', None, 'th', 'tw'), may hold values from -6 to 6
- text_states: bfloat16 [2, 256, 3072], P('cfg'), may hold values from -6 to 6
- text_count: int32 [2], P('cfg'), may hold values from 32 to 256, as said below
- guidance: float32 [1], replicated, may hold values from 4 to 7
- window_offsets: int32 [24, 2], P('hd'), may hold values from -1 to 1
- w_qkv: bfloat16 [3072, 3, 3072], P(('cfg', 'th', 'tw'), None, 'hd'), may hold values from -0.109375 to 0.109375
- q_gain: float32 [24, 128], P('hd'), may hold values from 1 to 2.5
- k_gain: float32 [24, 128], P('hd'), may hold values from 1 to 2.5
- w_out: bfloat16 [3072, 3072], P('hd', ('cfg', 'th', 'tw')), may hold values from -0.109375 to 0.109375
Outputs:
- guided: bfloat16 [6, 32, 64, 3072], P(None, 'th', 'tw', ('cfg', 'hd'))
Inputs may be any that keep to these rules, and one draw needn't show every extreme that they name: `text_count`: one of the two branches has all 256 text tokens valid.
All inputs are finite; a program needn't handle non-finite values.
Results may differ from a plain program's by a relative error of at most 0.0085.
The roundings to bfloat16 on the way count: a program that leaves them out, or rounds other values in their place, can miss the bound.
Values may be sent and summed in bfloat16 or wider, within the bound.
A program may use at most 128 MiB of HBM per device.

v0:
```python
import jax
import jax.numpy as jnp
from jax import lax
from jax.sharding import PartitionSpec as P


def extended(cells, sides, width):
    for axis, dim in sides:
        count = lax.axis_size(axis)
        ends = count - 1
        head = lax.slice_in_dim(cells, 0, width, axis=dim)
        tail = lax.slice_in_dim(cells, cells.shape[dim] - width, cells.shape[dim], axis=dim)
        cells = jnp.concatenate(
            [
                lax.ppermute(tail, axis, [(i, (i + 1) % count) for i in range(ends)]),
                cells,
                lax.ppermute(head, axis, [((i + 1) % count, i) for i in range(ends)]),
            ],
            axis=dim,
        )
    return cells


def scaled_norm(values, gain):
    mean_square = jnp.mean(values * values, axis=-1, keepdims=True)
    return values * lax.rsqrt(mean_square + 1e-06) * gain


def attend(queries, keys, values, text_keys, text_values, count):
    factor = 1.0 / queries.shape[-1] ** 0.5
    scores = jnp.einsum("qd,kd->qk", queries, keys, preferred_element_type=jnp.float32) * factor
    text_scores = (
        jnp.einsum("qd,kd->qk", queries, text_keys, preferred_element_type=jnp.float32) * factor
    )
    valid = jnp.arange(text_keys.shape[0], dtype=jnp.int32) < count
    expo = jnp.exp(scores)
    text_expo = jnp.where(valid[None, :], jnp.exp(text_scores), 0.0)
    total = jnp.sum(expo, axis=1, keepdims=True) + jnp.sum(text_expo, axis=1, keepdims=True)
    probs = (expo / total).astype(jnp.bfloat16)
    text_probs = (text_expo / total).astype(jnp.bfloat16)
    result = jnp.dot(probs, values, preferred_element_type=jnp.float32)
    result = result + jnp.dot(text_probs, text_values, preferred_element_type=jnp.float32)
    return result.astype(jnp.bfloat16)


def body(video, text_states, text_count, guidance, window_offsets, w_qkv, q_gain, k_gain, w_out):
    n_frames, local_rows, local_cols, model_width = video.shape[1:]
    head_local, head_size = q_gain.shape
    group_width = head_local * head_size
    token_count = n_frames * local_rows * local_cols
    flat_rows = video.reshape(token_count, model_width)
    text_rows = text_states[0]
    text_slots = text_rows.shape[0]
    weight_piece = lax.all_gather(w_qkv, ("cfg", "th", "tw"), axis=0, tiled=True)
    span = weight_piece.shape[0]
    video_part = jnp.dot(
        flat_rows, weight_piece.reshape(span, 3 * group_width), preferred_element_type=jnp.float32
    )
    text_part = jnp.dot(
        text_rows,
        weight_piece[:, 1:].reshape(span, 2 * group_width),
        preferred_element_type=jnp.float32,
    )
    proj = video_part
    text_proj = text_part
    proj = proj.reshape(token_count, 3, head_local, head_size)
    queries = scaled_norm(proj[:, 0], q_gain).astype(jnp.bfloat16)
    keys = scaled_norm(proj[:, 1], k_gain).astype(jnp.bfloat16)
    values = proj[:, 2].astype(jnp.bfloat16)
    text_proj = text_proj.reshape(text_slots, 2, head_local, head_size)
    text_keys = scaled_norm(text_proj[:, 0], k_gain).astype(jnp.bfloat16)
    text_values = text_proj[:, 1].astype(jnp.bfloat16)
    key_value = jnp.concatenate(
        [
            keys.reshape(n_frames, local_rows, local_cols, group_width),
            values.reshape(n_frames, local_rows, local_cols, group_width),
        ],
        axis=-1,
    )
    padded = extended(key_value, (("th", 1), ("tw", 2)), 16)
    tiles_down = local_rows // 8
    tiles_across = local_cols // 8
    grid_rows = tiles_down * lax.axis_size("th")
    grid_cols = tiles_across * lax.axis_size("tw")
    first_row = lax.axis_index("th") * tiles_down
    first_col = lax.axis_index("tw") * tiles_across
    query_grid = queries.reshape(n_frames, local_rows, local_cols, head_local, head_size)
    count = text_count[0]

    def pair_output(pair_index):
        head = pair_index // (tiles_down * tiles_across)
        tile_index = pair_index % (tiles_down * tiles_across)
        row_tile = tile_index // tiles_across
        col_tile = tile_index % tiles_across
        offset = lax.dynamic_index_in_dim(window_offsets, head, 0, False)
        center_row = jnp.clip(first_row + row_tile + offset[0], 1, grid_rows - 2)
        center_col = jnp.clip(first_col + col_tile + offset[1], 1, grid_cols - 2)
        zero = jnp.zeros((), jnp.int32)
        tile_q = lax.dynamic_slice(
            query_grid,
            (zero, row_tile * 8, col_tile * 8, head, zero),
            (n_frames, 8, 8, 1, head_size),
        )
        rim_row = (center_row + 1 - first_row) * 8
        rim_col = (center_col + 1 - first_col) * 8
        tile_k = lax.dynamic_slice(
            padded, (zero, rim_row, rim_col, head * head_size), (n_frames, 24, 24, head_size)
        )
        tile_v = lax.dynamic_slice(
            padded,
            (zero, rim_row, rim_col, group_width + head * head_size),
            (n_frames, 24, 24, head_size),
        )
        head_tk = lax.dynamic_index_in_dim(text_keys, head, 1, False)
        head_tv = lax.dynamic_index_in_dim(text_values, head, 1, False)
        return attend(
            tile_q.reshape(-1, head_size),
            tile_k.reshape(-1, head_size),
            tile_v.reshape(-1, head_size),
            head_tk,
            head_tv,
            count,
        )

    outputs = lax.map(
        pair_output, jnp.arange(head_local * tiles_down * tiles_across, dtype=jnp.int32)
    )
    outputs = outputs.reshape(head_local, tiles_down, tiles_across, n_frames, 8, 8, head_size)
    attended = jnp.transpose(outputs, (3, 1, 4, 2, 5, 0, 6)).reshape(token_count, group_width)
    scale_value = guidance[0]
    branch_weight = jnp.where(lax.axis_index("cfg") == 0, scale_value, 1.0 - scale_value)
    partial_terms = branch_weight * jnp.dot(
        attended,
        lax.all_gather(w_out, ("cfg", "th", "tw"), axis=1, tiled=True),
        preferred_element_type=jnp.float32,
    )
    summed = lax.psum_scatter(partial_terms, ("cfg", "hd"), scatter_dimension=1, tiled=True)
    return summed.astype(jnp.bfloat16).reshape(n_frames, local_rows, local_cols, summed.shape[-1])


def solution(mesh):
    return jax.shard_map(
        body,
        mesh=mesh,
        in_specs=(
            P("cfg", None, "th", "tw", None),
            P("cfg", None, None),
            P("cfg"),
            P(),
            P("hd", None),
            P(("cfg", "th", "tw"), None, "hd"),
            P("hd", None),
            P("hd", None),
            P("hd", ("cfg", "th", "tw")),
        ),
        out_specs=P(None, "th", "tw", ("cfg", "hd")),
        check_vma=False,
    )
```

profile of v0, /device:TPU:1, one launch (start us, length us, event | category | flops | bytes accessed | tf_op | source)
XLA Modules:
  0.0 696.0 jit_solution(14583963810313454957)
XLA Ops:
  7.3 59.2 %all-gather.3.cloned.1.call-done = bf16[3072,3,384]{2,0,1:T(8,128)(2,1)} async-done(((bf16[192,3,384]{2,0,1:T(8,128)(2,1)}), bf16[3072,3,384]{2,0,1:T(8,128)(2,1)}) %all-gather.3.cloned.1.call-update) | async-done | bytes 7077904 | tf_op jit(solution)/shard_map/all_gather | solution.py:54
  66.5 10.3 %copy.29 = bf16[3072,3,384]{0,2,1:T(8,128)(2,1)} copy(bf16[3072,3,384]{2,0,1:T(8,128)(2,1)} %all-gather.3.cloned.1.call-done) | data formatting | bytes 14155776 | tf_op jit(solution)/shard_map/all_gather | solution.py:54
  76.8 16.0 %fusion.20 = f32[1536,3,3,128]{3,0,2,1:T(8,128)S(1)} fusion(bf16[1536,3072,1,1]{1,0,3,2:T(8,128)(2,1)} %bitcast.112, bf16[3,3,128,3072]{3,2,1,0:T(8,128)(2,1)} %bitcast.106), kind=kOutput, calls=%fused_computation.46 | convolution fusion | flops 10871635968 | bytes 23592960 | tf_op jit(solution)/shard_map/dot_general | solution.py:56
  92.9 3.3 multiply_reduce_fusion
  96.2 8.3 %copy.32 = bf16[1536,1,3,128]{3,2,0,1:T(4,128)(2,1)} copy(bf16[1536,1,3,128]{3,0,2,1:T(8,128)(2,1)S(1)} %slice.59) | data formatting | bytes 2359296 | tf_op jit(solution)/shard_map/slice | solution.py:69
  104.5 3.4 convert_element_type.46
  108.5 1.0 copy.31
  109.5 3.2 mul.138
  112.7 4.9 mul.139
  117.6 7.8 %copy.30 = f32[1536,1,3,128]{3,2,0,1:T(4,128)} copy(f32[1536,1,3,128]{3,0,2,1:T(8,128)} %get-tuple-element.268) | data formatting | bytes 4718592 | tf_op jit(solution)/shard_map/slice | solution.py:68
  125.4 4.9 squeeze.61
  130.3 2.7 multiply_convert_fusion
  133.2 2.4 collective-permute-start.1
  135.6 1.3 collective-permute-start
  136.9 2.7 collective-permute-done.1
  139.6 2.4 collective-permute-done
  142.1 3.6 pad_maximum_fusion.1
  145.7 1.3 collective-permute-start.3
  147.0 6.9 collective-permute-start.2
  154.6 4.8 slice.45
  159.6 3.9 fusion.14
  163.7 1.9 multiply_convert_fusion.1
  165.6 148.0 %collective-permute-done.3 = bf16[6,48,16,768]{3,2,1,0:T(8,128)(2,1)} collective-permute-done((bf16[6,48,16,768]{3,2,1,0:T(8,128)(2,1)}, bf16[6,48,16,768]{3,2,1,0:T(8,128)(2,1)}, u32[]{:S(2)}, u32[]{:S(2)}) %collective-permute-start.3) | collective-permute-done | bytes 7077920 | tf_op jit(solution)/shard_map/ppermute | solution.py:17
  314.5 13.7 %pad_maximum_fusion = bf16[6,48,48,768]{3,2,1,0:T(8,128)(2,1)} fusion(bf16[6,48,16,768]{3,2,1,0:T(8,128)(2,1)} %collective-permute-done.3, bf16[6,16,16,768]{3,2,1,0:T(8,128)(2,1)S(1)} %copy-done.6, bf16[6,16,16,384]{3,2,1,0:T(8,128)(2,1)S(1)} %convert_element_type.46, bf16[6,16,16,384]{3,2,1,0:T(8,128)(2,1)S(1)} %copy-done.3, ...), kind=kLoop, calls=%fused_computation.24 | loop fusion | flops 127401984 | bytes 42467328 | tf_op jit(solution)/shard_map/concatenate | solution.py:13
  328.2 135.6 %while.13 = (s32[]{:T(128)}, bf16[12,384,128]{2,1,0:T(8,128)(2,1)}, s32[12]{0:T(128)S(1)}, bf16[6,16,16,3,128]{4,2,1,0,3:T(8,128)(2,1)}, s32[]{:T(128)}, /*index...) while((s32[]{:T(128)}, bf16[12,384,128]{2,1,0:T(8,128)(2,1)}, ...), condition=%wide.region_6.7_spmd, body=%wide.region_3.6_spmd.sunk | while | flops 735707072 | bytes 17740668 | solution.py:125
  334.8 1.8 constant_dynamic-slice_fusion.8
  336.6 1.0 fusion.46
  337.6 0.9 fusion.48
  346.1 1.8 constant_dynamic-slice_fusion.8
  347.9 1.0 fusion.46
  348.9 0.9 fusion.48
  357.4 1.8 constant_dynamic-slice_fusion.8
  359.2 1.0 fusion.46
  360.2 0.9 fusion.48
  368.7 1.8 constant_dynamic-slice_fusion.8
  370.5 1.0 fusion.46
  380.0 1.8 constant_dynamic-slice_fusion.8
  381.8 1.0 fusion.46
  382.8 0.9 fusion.48
  391.3 1.8 constant_dynamic-slice_fusion.8
  393.1 1.0 fusion.46
  402.6 1.8 constant_dynamic-slice_fusion.8
  404.4 1.0 fusion.46
  405.4 0.9 fusion.48
  413.9 1.8 constant_dynamic-slice_fusion.8
  415.7 1.0 fusion.46
  416.7 0.9 fusion.48
  425.2 1.8 constant_dynamic-slice_fusion.8
  427.0 1.0 fusion.46
  428.0 0.9 fusion.48
  436.5 1.8 constant_dynamic-slice_fusion.8
  438.3 1.0 fusion.46
  439.3 0.9 fusion.48
  447.8 1.8 constant_dynamic-slice_fusion.8
  449.6 1.0 fusion.46
  450.6 0.9 fusion.48
  459.0 1.8 constant_dynamic-slice_fusion.8
  460.9 1.0 fusion.46
  461.9 0.9 fusion.48
  463.7 1.5 copy.36
  465.2 10.9 %convolution_multiply_fusion.2 = f32[1536,3072]{0,1:T(8,128)} fusion(bf16[1536,384]{1,0:T(8,128)(2,1)S(1)} %bitcast.108, bf16[384,3072]{0,1:T(8,128)(2,1)} %all-gather.5.cloned.1.call-done, f32[]{:T(128)S(6)} %select_n.106), kind=kOutput, calls=%fused_computation.25 | convolution fusion | flops 3628597248 | bytes 22413316 | tf_op jit(solution)/shard_map/dot_general | solution.py:132
  476.2 210.7 %reduce-scatter.2.cloned.1.call-done = f32[1536,192]{0,1:T(8,128)} async-done(((f32[1536,3072]{0,1:T(8,128)}), f32[1536,192]{0,1:T(8,128)}) %reduce-scatter.2.cloned.1.call-update) | async-done | bytes 1179664 | tf_op jit(solution)/shard_map/reduce_scatter | solution.py:137
  686.9 1.3 convert_element_type.49
  688.3 1.2 copy.37
  (140 shorter events, 52.9 us)
Async XLA Ops:
  6.5 153.0 %copy-start = (bf16[1,256,3072]{2,1,0:T(8,128)(2,1)S(1)}, bf16[1,256,3072]{2,1,0:T(8,128)(2,1)}, u32[]{:S(2)}) copy-start(bf16[1,256,3072]{2,1,0:T(8,128)(2,1)} %param.12) | copy-start | bytes 4718596
  6.5 59.9 %all-gather.3.cloned.1.call-start = ((), (), s32[]{:S(2)}) async-start(), calls=%async_computation.1 | async-start | bytes 7520256 | tf_op jit(solution)/shard_map/all_gather | solution.py:54
  7.3 458.0 %all-gather.5.cloned.1.call-start = ((), (), s32[]{:S(2)}) async-start(), calls=%async_computation.2 | async-start | bytes 2506752 | tf_op jit(solution)/shard_map/all_gather | solution.py:134
  117.6 12.7 %copy-start.10 = (f32[3,128]{1,0:T(4,128)S(1)}, f32[3,128]{1,0:T(4,128)}, u32[]{:S(2)}) copy-start(f32[3,128]{1,0:T(4,128)} %param.18) | copy-start | bytes 4612
  133.0 12.7 %copy-start.2 = (bf16[6,16,16,384]{3,2,1,0:T(8,128)(2,1)}, bf16[6,16,16,384]{3,2,1,0:T(8,128)(2,1)S(1)}, u32[]{:S(2)}) copy-start(bf16[6,16,16,384]{3,2,1,0:T(8,128)(2,1)S(1)} %multiply_convert_fusion) | copy-start | bytes 3538948
  133.2 6.4 collective-permute-start.1
  135.6 6.4 collective-permute-start
  139.6 6.1 copy-start.5
  142.1 3.6 copy-start.7
  145.7 167.9 %collective-permute-start.3 = (bf16[6,48,16,768]{3,2,1,0:T(8,128)(2,1)}, bf16[6,48,16,768]{3,2,1,0:T(8,128)(2,1)}, u32[]{:S(2)}, u32[]{:S(2)}) collective-permute-start(bf16[6,48,16,768]{3,2,1,0:T(8,128)(2,1)} %pad_maximum_fusion.1), channel_id=1, source_target_pairs={{8,0},{16,8},{24,16},{9,1},{17,9},{25,17},{10,2},{18,10},{26,18},{... | collective-permute-start | bytes 21233672 | tf_op jit(solution)/shard_map/ppermute | solution.py:17
  147.0 167.5 %collective-permute-start.2 = (bf16[6,48,16,768]{3,2,1,0:T(8,128)(2,1)}, bf16[6,48,16,768]{3,2,1,0:T(8,128)(2,1)}, u32[]{:S(2)}, u32[]{:S(2)}) collective-permute-start(bf16[6,48,16,768]{3,2,1,0:T(8,128)(2,1)} %pad_maximum_fusion.1), channel_id=1, source_target_pairs={{0,8},{8,16},{16,24},{1,9},{9,17},{17,25},{2,10},{10,18},{18,26},{... | collective-permute-start | bytes 21233672 | tf_op jit(solution)/shard_map/ppermute | solution.py:15
  153.9 533.0 %reduce-scatter.2.cloned.1.call-start = ((), (), s32[]{:S(2)}) async-start(), calls=%async_computation.3 | async-start | bytes 20054016 | tf_op jit(solution)/shard_map/reduce_scatter | solution.py:137
  154.6 4.8 copy-start.8
  159.5 4.2 copy-start.4
  159.6 4.2 copy-start.11
  163.5 151.0 %copy-start.3 = (bf16[6,16,16,384]{3,2,1,0:T(8,128)(2,1)S(1)}, bf16[6,16,16,384]{3,2,1,0:T(8,128)(2,1)}, u32[]{:S(2)}) copy-start(bf16[6,16,16,384]{3,2,1,0:T(8,128)(2,1)} %copy-done.2) | copy-start | bytes 3538948
  163.5 151.0 %copy-start.6 = (bf16[6,16,16,768]{3,2,1,0:T(8,128)(2,1)S(1)}, bf16[6,16,16,768]{3,2,1,0:T(8,128)(2,1)}, u32[]{:S(2)}) copy-start(bf16[6,16,16,768]{3,2,1,0:T(8,128)(2,1)} %copy-done.5) | copy-start | bytes 7077892
  165.6 162.6 %copy-start.9 = (s32[3,2]{0,1:T(2,128)S(1)}, s32[3,2]{0,1:T(2,128)}, u32[]{:S(2)}) copy-start(s32[3,2]{0,1:T(2,128)} %param.15) | copy-start | bytes 76
  476.2 213.3 %copy-start.1 = (bf16[1,256,3072]{2,1,0:T(8,128)(2,1)S(1)}, bf16[1,256,3072]{2,1,0:T(8,128)(2,1)}, u32[]{:S(2)}) copy-start(bf16[1,256,3072]{2,1,0:T(8,128)(2,1)} %param.12) | copy-start | bytes 4718596
Sparse Core Ops, SparseCore 0:
  9.0 57.4 all-gather.2
  154.0 55.9 all-gather.4
  476.3 210.5 reduce-scatter.1
where the time goes:
time: 698 us; the launch traced here: 696 us
  waiting for transfers between devices  425 us (61%)
  local copies, waits for them, and re-layouts  98.8 us (14%)
  matrix products  68.4 us (10%)
  loops' own time  42.6 us (6%)
  other arithmetic  35.4 us (5%)
  between operations  14 us (2%)
  starting transfers between devices  11.9 us (2%)
    reduce_scatter x1, waiting for transfers between devices, body(): lax.psum_scatter(partial_terms, ('cfg', 'hd'), scatter_dimension=1, tiled...  211 us
    ppermute x2, waiting for transfers between devices, extended(): lax.ppermute(head, axis, [((i + 1) % count, i) for i in range(ends)])  151 us
    all_gather x1, waiting for transfers between devices, body(): lax.all_gather(w_qkv, ('cfg', 'th', 'tw'), axis=0, tiled=True)  59.2 us
    another operation x1, loops' own time, body(): lax.map(pair_output, jnp.arange(head_local * tiles_down * tiles_across, d...  42.6 us
    dynamic_slice x12, local copies, waits for them, and re-layouts, pair_output(): lax.dynamic_slice(padded, (zero, rim_row, rim_col, head * head_size), (n_...  21.7 us
    concatenate x2, other arithmetic, extended(): jnp.concatenate([lax.ppermute(tail, axis, [(i, (i + 1) % count) for i in...  17.3 us
    dot_general x1, matrix products, body(): jnp.dot(flat_rows, weight_piece.reshape(span, 3 * group_width), preferred...  16 us
  transfers between devices with their start and end apart: 7, of which 6 were waited for; matrix products, arithmetic and copies ran while one was open for 17% of the time, Pallas kernels for 0%

commit v1 on v0

v1 whole, which is shorter than its diff:
```python
import functools
import math

import jax
import jax.numpy as jnp
from jax import lax
from jax.experimental import pallas as pl
from jax.experimental.pallas import tpu as pltpu
from jax.sharding import PartitionSpec as P

MESH = pl.DeviceIdType.MESH
BF = jnp.bfloat16
F32 = jnp.float32
VMEM = pl.BlockSpec(memory_space=pltpu.VMEM)
SMEM = pl.BlockSpec(memory_space=pltpu.SMEM)
ANY = pl.BlockSpec(memory_space=pl.ANY)
LIMIT = 62 << 20
TILE = 384
TOK = 1536


def place():
    c, t, w, h = (lax.axis_index(a) for a in ("cfg", "th", "tw", "hd"))
    return c, t, w, h // 4, lax.rem(h, 4)


def partners():
    c, t, w, x, y = place()
    return {
        "left": {"tw": lax.rem(w + 3, 4)},
        "right": {"tw": lax.rem(w + 1, 4)},
        "core": {"th": 1 - t},
        "xl": {"cfg": 1 - c},
        "xh": {"hd": (1 - x) * 4 + y},
        "xd": {"cfg": 1 - c, "hd": (1 - x) * 4 + y},
        "up": {"hd": x * 4 + lax.rem(y + 1, 4)},
        "down": {"hd": x * 4 + lax.rem(y + 3, 4)},
    }


def greet(names):
    to = partners()
    barrier = pltpu.get_barrier_semaphore()
    for name in names:
        pl.semaphore_signal(barrier, inc=1, device_id=to[name], device_id_type=MESH)
    pl.semaphore_wait(barrier, len(names))


class Mail:
    def __init__(self, send, recv):
        self.send, self.recv, self.n, self.all = send, recv, 0, []
        self.to = partners()

    def copy(self, src, dst, name):
        k = self.n
        self.n += 1
        cp = pltpu.make_async_remote_copy(
            src_ref=src,
            dst_ref=dst,
            send_sem=self.send.at[k],
            recv_sem=self.recv.at[k],
            device_id=self.to[name],
            device_id_type=MESH,
        )
        self.all.append(cp)
        return cp

    def post(self, src, dst, name):
        cp = self.copy(src, dst, name)
        cp.start()
        return cp

    def close(self):
        for cp in self.all:
            cp.wait_send()


def normed(v, gain):
    ms = jnp.mean(v * v, axis=-1, keepdims=True)
    return v * lax.rsqrt(ms + 1e-06) * gain


GROUP_PIECES = (((1, 0), (2, 0)), ((1, 1), (2, 1)), ((1, 2), (2, 2)), ((0, 0), (0, 1)), ((0, 2),))
N_GROUPS = len(GROUP_PIECES)
N_MAIL1 = N_GROUPS * 16 + 8


def project_kernel(
    video, wq, wo, text, qg, kg, q_out, kv_out, tkv_out, wo_out, xv, tv, wv0, wv1, wv2, wv3, wv4, wov, lsem, ssem, rsem
):
    c, t, w, x, y = place()
    wv = (wv0, wv1, wv2, wv3, wv4)
    half = 768
    loads = [
        pltpu.make_async_copy(video.at[pl.ds(i * half, half)], xv.at[pl.ds(i * half, half)], lsem.at[i])
        for i in range(2)
    ]
    loads.append(pltpu.make_async_copy(text, tv, lsem.at[2]))

    def rows(cc, tt, ww):
        return pl.ds(pl.multiple_of((cc * 8 + tt * 4 + ww) * 192, 64), 192)

    own = rows(c, t, w)
    w_loads = []
    n = 3
    for g, pieces in enumerate(GROUP_PIECES):
        for k, (part, h) in enumerate(pieces):
            cp = pltpu.make_async_copy(
                wq.at[:, pl.ds(part * 384 + h * 128, 128)], wv[g].at[own, pl.ds(k * 128, 128)], lsem.at[n]
            )
            n += 1
            cp.start()
            w_loads.append(cp)
    wo_load = pltpu.make_async_copy(wo, wov.at[w], lsem.at[n])
    wo_load.start()
    for cp in loads:
        cp.start()
    greet(("left", "right", "xl", "core"))
    for cp in w_loads:
        cp.wait()
    mail = Mail(ssem, rsem)
    wl, wr, w2 = lax.rem(w + 3, 4), lax.rem(w + 1, 4), lax.rem(w + 2, 4)
    state = [None] * N_GROUPS

    def half_rows(cc, tt, ww, k):
        return pl.ds(pl.multiple_of((cc * 8 + tt * 4 + ww) * 192 + k * 96, 32), 96)

    def start_own(g):
        ref = wv[g]
        s = {}
        for name in ("left", "right", "xl", "core"):
            s[name] = mail.post(ref.at[own], ref.at[own], name)
        state[g] = s

    def z_events(g):
        ref, s = wv[g], state[g]
        s["right"].wait_recv()
        r = half_rows(c, t, wl, 0)
        s["r2"] = mail.post(ref.at[r], ref.at[r], "right")
        r = rows(c, t, wl)
        s["x1"] = mail.post(ref.at[r], ref.at[r], "xl")
        s["c1"] = mail.post(ref.at[r], ref.at[r], "core")
        s["left"].wait_recv()
        r = half_rows(c, t, wr, 1)
        s["l2"] = mail.post(ref.at[r], ref.at[r], "left")
        r = rows(c, t, wr)
        s["x2"] = mail.post(ref.at[r], ref.at[r], "xl")
        s["c2"] = mail.post(ref.at[r], ref.at[r], "core")
        s["r2"].wait_recv()
        s["l2"].wait_recv()
        r = rows(c, t, w2)
        s["x3"] = mail.post(ref.at[r], ref.at[r], "xl")
        s["c3"] = mail.post(ref.at[r], ref.at[r], "core")

    def x_events(g):
        ref, s = wv[g], state[g]
        for k, (key, ww) in enumerate((("xl", w), ("x1", wl), ("x2", wr), ("x3", w2))):
            s[key].wait_recv()
            r = rows(1 - c, t, ww)
            s["d%d" % k] = mail.post(ref.at[r], ref.at[r], "core")
        for key in ("core", "c1", "c2", "c3", "d0", "d1", "d2", "d3"):
            s[key].wait_recv()

    def multiply(g):
        ref, pieces = wv[g], GROUP_PIECES[g]

        def step(mc, carry):
            acc = jnp.dot(
                xv[pl.ds(pl.multiple_of(mc * half, half), half), :], ref[...], preferred_element_type=F32
            )
            for k, (part, h) in enumerate(pieces):
                v = acc[:, k * 128 : (k + 1) * 128]
                if part < 2:
                    v = normed(v, (qg if part == 0 else kg)[h : h + 1, :])
                v = v.reshape(3, 2, 8, 2, 8, 128)
                for i in range(2):
                    for j in range(2):
                        tile = v[:, i, :, j].reshape(192, 128).astype(BF)
                        if part == 0:
                            q_out[h, i * 2 + j, pl.ds(pl.multiple_of(mc * 192, 64), 192), :] = tile
                        else:
                            kv_out[h, j, part - 1, i, pl.ds(pl.multiple_of(mc * 192, 64), 192), :] = tile
            return carry

        lax.fori_loop(0, 2, step, 0)
        if pieces[0][0] == 1:
            h = pieces[0][1]
            acc = jnp.dot(tv[...], ref[...], preferred_element_type=F32)
            tkv_out[h, 0] = normed(acc[:, :128], kg[h : h + 1, :]).astype(BF)
            tkv_out[h, 1] = acc[:, 128:].astype(BF)

    start_own(0)
    start_own(1)
    z_events(0)
    for g in range(N_GROUPS):
        if g + 2 < N_GROUPS:
            start_own(g + 2)
        if g + 1 < N_GROUPS:
            z_events(g + 1)
        if g == 2:
            wo_load.wait()
            o_left = mail.post(wov.at[w], wov.at[w], "left")
            o_right = mail.post(wov.at[w], wov.at[w], "right")
        if g == 3:
            o_right.wait_recv()
            o_r2 = mail.post(wov.at[wl, pl.ds(0, 96)], wov.at[wl, pl.ds(0, 96)], "right")
            o_left.wait_recv()
            o_l2 = mail.post(wov.at[wr, pl.ds(96, 96)], wov.at[wr, pl.ds(96, 96)], "left")
        x_events(g)
        if g == 0:
            for cp in loads:
                cp.wait()
        multiply(g)
    o_r2.wait_recv()
    o_l2.wait_recv()
    wo_out[...] = wov[...]
    mail.close()


def project(video, wq, wo, text, qg, kg):
    return pl.pallas_call(
        project_kernel,
        out_shape=(
            jax.ShapeDtypeStruct((3, 4, TILE, 128), BF),
            jax.ShapeDtypeStruct((3, 2, 2, 2, TILE, 128), BF),
            jax.ShapeDtypeStruct((3, 2, 256, 128), BF),
            jax.ShapeDtypeStruct((4, 192, 384), BF),
        ),
        in_specs=[ANY, ANY, ANY, ANY, VMEM, VMEM],
        out_specs=(VMEM, VMEM, VMEM, VMEM),
        scratch_shapes=[
            pltpu.VMEM((TOK, 3072), BF),
            pltpu.VMEM((256, 3072), BF),
            pltpu.VMEM((3072, 256), BF),
            pltpu.VMEM((3072, 256), BF),
            pltpu.VMEM((3072, 256), BF),
            pltpu.VMEM((3072, 256), BF),
            pltpu.VMEM((3072, 128), BF),
            pltpu.VMEM((4, 192, 384), BF),
            pltpu.SemaphoreType.DMA((16,)),
            pltpu.SemaphoreType.DMA((N_MAIL1,)),
            pltpu.SemaphoreType.DMA((N_MAIL1,)),
        ],
        compiler_params=pltpu.CompilerParams(collective_id=0, has_side_effects=True, vmem_limit_bytes=LIMIT),
    )(video, wq, wo, text, qg, kg)


SCALE = math.log2(math.e) / math.sqrt(128.0)


def attend_tile(q, kvb, p0, r0, tk, tv, count):
    def weights(keys):
        s = lax.dot_general(q, keys, (((1,), (1,)), ((), ())), preferred_element_type=F32)
        return jnp.exp2(s * SCALE)

    p = weights(tk)
    valid = lax.broadcasted_iota(jnp.int32, p.shape, 1) < count
    p = jnp.where(valid, p, 0.0)
    den = jnp.sum(p, axis=1, keepdims=True)
    acc = jnp.dot(p.astype(BF), tv, preferred_element_type=F32)
    span = pl.ds(r0, 3)
    for d in range(3):
        p = weights(kvb[p0 + d, 0, span].reshape(3 * TILE, 128))
        den = den + jnp.sum(p, axis=1, keepdims=True)
        acc = acc + jnp.dot(p.astype(BF), kvb[p0 + d, 1, span].reshape(3 * TILE, 128), preferred_element_type=F32)
    return (acc / den).astype(BF)


N_MAIL2 = 3 * 9 + 8


def attend_kernel(q, kv, tkv, wo, off, cnt, att, wt, kvb0, kvb1, kvb2, lsem, ssem, rsem):
    c, t, w, x, y = place()
    kvb = (kvb0, kvb1, kvb2)
    mine = pl.ds(2 * t, 2)
    lanes = pl.ds(pl.multiple_of(x * 384, 128), 384)
    local = [pltpu.make_async_copy(kv.at[h], kvb[h].at[pl.ds(2, 2), :, mine], lsem.at[h]) for h in range(3)]
    local.append(pltpu.make_async_copy(wo, wt.at[:, c, t, :, lanes], lsem.at[3]))
    for cp in local:
        cp.start()
    greet(("left", "right", "core", "xl", "xh", "xd"))
    mail = Mail(ssem, rsem)
    halo = []
    for h in range(3):
        b = kvb[h]
        halo.append(
            (
                mail.post(kv.at[h, 0], b.at[4, :, mine], "left"),
                mail.post(kv.at[h, 1], b.at[1, :, mine], "right"),
                mail.post(kv.at[h, 1], b.at[5, :, mine], "left"),
                mail.post(kv.at[h, 0], b.at[0, :, mine], "right"),
                mail.post(kv.at[h], b.at[pl.ds(2, 2), :, mine], "core"),
            )
        )
        if h == 0:
            wo_own = mail.post(wo, wt.at[:, c, t, :, lanes], "core")
            wo_x = [mail.post(wo, wt.at[:, c, t, :, lanes], name) for name in ("xl", "xh", "xd")]

    count = cnt[0]
    for h in range(3):
        b = kvb[h]
        relayed = []
        for k, p in enumerate((4, 1, 5, 0)):
            halo[h][k].wait_recv()
            relayed.append(mail.post(b.at[p, :, mine], b.at[p, :, mine], "core"))
        if h == 1:
            wo_core = []
            for cp, (cc, xx) in zip(wo_x, ((1 - c, x), (c, 1 - x), (1 - c, 1 - x))):
                cp.wait_recv()
                at = wt.at[:, cc, t, :, pl.ds(pl.multiple_of(xx * 384, 128), 384)]
                wo_core.append(mail.post(at, at, "core"))
        halo[h][4].wait_recv()
        for cp in relayed:
            cp.wait_recv()
        local[h].wait()

        def tile(k, carry):
            i, j = k // 2, lax.rem(k, 2)
            row = jnp.clip(2 * t + i + off[h, 0], 1, 2) - 1
            col = jnp.clip(2 * w + j + off[h, 1], 1, 6) + 1 - 2 * w
            att[k, :, h * 128 : (h + 1) * 128] = attend_tile(q[h, k], b, col, row, tkv[h, 0], tkv[h, 1], count)
            return carry

        lax.fori_loop(0, 4, tile, 0)
    local[3].wait()
    wo_own.wait_recv()
    for cp in wo_core:
        cp.wait_recv()
    mail.close()


def attention(q, kv, tkv, wo, off, cnt):
    return pl.pallas_call(
        attend_kernel,
        out_shape=(
            jax.ShapeDtypeStruct((4, TILE, 384), BF),
            jax.ShapeDtypeStruct((4, 2, 2, 192, 768), BF),
        ),
        in_specs=[VMEM, VMEM, VMEM, VMEM, SMEM, SMEM],
        out_specs=(VMEM, VMEM),
        scratch_shapes=[
            pltpu.VMEM((6, 2, 4, TILE, 128), BF),
            pltpu.VMEM((6, 2, 4, TILE, 128), BF),
            pltpu.VMEM((6, 2, 4, TILE, 128), BF),
            pltpu.SemaphoreType.DMA((4,)),
            pltpu.SemaphoreType.DMA((N_MAIL2,)),
            pltpu.SemaphoreType.DMA((N_MAIL2,)),
        ],
        compiler_params=pltpu.CompilerParams(collective_id=1, has_side_effects=True, vmem_limit_bytes=LIMIT),
    )(q, kv, tkv, wo, off, cnt)


def output_kernel(att, wt, guide, out, box, comb, s1, sent, got, mid, ends, lsem, ssem, rsem):
    c, t, w, x, y = place()
    greet(("xl", "xh", "xd", "up", "down"))
    mail = Mail(ssem, rsem)
    spot = c * 2 + x
    peers = (("xl", 1 - c, x), ("xh", c, 1 - x), ("xd", 1 - c, 1 - x))
    keep = pltpu.make_async_copy(att.at[spot], box.at[spot], lsem.at[0])
    keep.start()
    ins = [mail.post(att.at[cc * 2 + xx], box.at[spot], name) for name, cc, xx in peers]
    keep.wait()
    for cp in ins:
        cp.wait_recv()
    g = guide[0]
    for xx in range(2):
        mixed = g * box[xx].astype(F32) + (1.0 - g) * box[2 + xx].astype(F32)
        comb[:, xx * 384 : (xx + 1) * 384] = mixed.astype(BF)

    def term(yy, half):
        a = comb[...]
        parts = wt[yy, half].reshape(384, 768)
        return lax.dot_general(a, parts, (((1,), (1,)), ((), ())), preferred_element_type=F32)

    far, up, down = lax.rem(y + 2, 4), lax.rem(y + 1, 4), lax.rem(y + 3, 4)
    sent[0] = term(far, 0).astype(BF)
    a1 = mail.post(sent.at[0], s1.at[0], "up")
    sent[1] = term(far, 1).astype(BF)
    a2 = mail.post(sent.at[1], s1.at[1], "down")
    sent[2] = term(up, 1).astype(BF)
    b1 = mail.post(sent.at[2], got.at[0], "up")
    sent[3] = term(down, 0).astype(BF)
    b2 = mail.post(sent.at[3], got.at[1], "down")
    t_up = term(up, 0)
    a1.wait_recv()
    sent[4] = (t_up + s1[0].astype(F32)).astype(BF)
    b3 = mail.post(sent.at[4], got.at[2], "up")
    t_down = term(down, 1)
    a2.wait_recv()
    sent[5] = (t_down + s1[1].astype(F32)).astype(BF)
    b4 = mail.post(sent.at[5], got.at[3], "down")
    own0 = term(y, 0)
    own1 = term(y, 1)
    b2.wait_recv()
    b3.wait_recv()
    total0 = own0 + got[1].astype(F32) + got[2].astype(F32)
    b1.wait_recv()
    b4.wait_recv()
    total1 = own1 + got[0].astype(F32) + got[3].astype(F32)
    for k in range(2):
        mid[0, k] = total0[:, k * 192 : (k + 1) * 192].astype(BF)
        mid[1, k] = total1[:, k * 192 : (k + 1) * 192].astype(BF)
    keep = pltpu.make_async_copy(mid.at[c, x], ends.at[spot], lsem.at[1])
    keep.start()
    outs = [mail.post(mid.at[cc, xx], ends.at[spot], name) for name, cc, xx in peers]
    keep.wait()
    for cp in outs:
        cp.wait_recv()
    for i in range(2):
        sides = [ends[i * 2 + j].astype(F32).reshape(6, 8, 8, 192) for j in range(2)]
        out[:, i * 8 : (i + 1) * 8] = jnp.concatenate(sides, axis=2).astype(BF)
    mail.close()


def finish(att, wt, guide):
    return pl.pallas_call(
        output_kernel,
        out_shape=jax.ShapeDtypeStruct((6, 16, 16, 192), BF),
        in_specs=[VMEM, VMEM, SMEM],
        out_specs=VMEM,
        scratch_shapes=[
            pltpu.VMEM((4, TILE, 384), BF),
            pltpu.VMEM((TILE, 768), BF),
            pltpu.VMEM((2, TILE, 384), BF),
            pltpu.VMEM((6, TILE, 384), BF),
            pltpu.VMEM((4, TILE, 384), BF),
            pltpu.VMEM((2, 2, TILE, 192), BF),
            pltpu.VMEM((4, TILE, 192), BF),
            pltpu.SemaphoreType.DMA((2,)),
            pltpu.SemaphoreType.DMA((12,)),
            pltpu.SemaphoreType.DMA((12,)),
        ],
        compiler_params=pltpu.CompilerParams(collective_id=2, has_side_effects=True, vmem_limit_bytes=LIMIT),
    )(att, wt, guide)


def body(video, text_states, text_count, guidance, window_offsets, w_qkv, q_gain, k_gain, w_out):
    q, kv, tkv, wo = project(
        video.reshape(TOK, 3072), w_qkv.reshape(192, 1152), w_out.T, text_states[0], q_gain, k_gain
    )
    att, wt = attention(q, kv, tkv, wo, window_offsets, text_count)
    return finish(att, wt, guidance)


def solution(mesh):
    return jax.shard_map(
        body,
        mesh=mesh,
        in_specs=(
            P("cfg", None, "th", "tw", None),
            P("cfg", None, None),
            P("cfg"),
            P(),
            P("hd", None),
            P(("cfg", "th", "tw"), None, "hd"),
            P("hd", None),
            P("hd", None),
            P("hd", ("cfg", "th", "tw")),
        ),
        out_specs=P(None, "th", "tw", ("cfg", "hd")),
        check_vma=False,
    )
```

time: 698 us -> 191 us (0.27)
  waiting for transfers between devices: 425 us -> 0 us
  Pallas kernels: 0 us -> 184 us
  local copies, waits for them, and re-layouts: 98.8 us -> 4.58 us
  matrix products: 68.4 us -> 0 us
  loops' own time: 42.6 us -> 0 us
  other arithmetic: 35.4 us -> 0 us
  between operations: 14 us -> 1.33 us
  starting transfers between devices: 11.9 us -> 0 us
    reduce_scatter x1 -> x0, waiting for transfers between devices: 211 us -> none  [body(): lax.psum_scatter(partial_terms, ('cfg', 'hd'), scatter_dimension=1, tiled...]
    pallas_call x0 -> x3, Pallas kernels: none -> 184 us  [the longest x1 70.4 us: attention(): pl.pallas_call(attend_kernel, out_shape=(jax.ShapeDtypeStruct((4, TILE, 3...]
    ppermute x4 -> x0, waiting for transfers between devices: 154 us -> none  [the longest x2 151 us: extended(): lax.ppermute(head, axis, [((i + 1) % count, i) for i in range(ends)])]
    dot_general x51 -> x0, matrix products: 68.4 us -> none  [the longest x1 16 us: body(): jnp.dot(flat_rows, weight_piece.reshape(span, 3 * group_width), preferred...]
    all_gather x2 -> x0, waiting for transfers between devices: 59.2 us -> none  [the longest x1 59.2 us: body(): lax.all_gather(w_qkv, ('cfg', 'th', 'tw'), axis=0, tiled=True)]
    another operation x1 -> x0, loops' own time: 42.6 us -> none  [body(): lax.map(pair_output, jnp.arange(head_local * tiles_down * tiles_across, d...]
    dynamic_slice x48 -> x0, local copies, waits for them, and re-layouts: 40.2 us -> none  [the longest x12 21.7 us: pair_output(): lax.dynamic_slice(padded, (zero, rim_row, rim_col, head * head_size), (n_...]
    slice x16 -> x0, local copies, waits for them, and re-layouts: 28.2 us -> none  [the longest x2 8.44 us: body(): values = proj[:, 2].astype(jnp.bfloat16)]
  transfers between devices with their start and end apart: 7 -> 0, of which waited for: 6 -> 0; matrix products, arithmetic and copies ran while one was open for 17% -> 0% of each run, Pallas kernels for 0% -> 0%
where the time goes in v1:
time: 191 us; the launch traced here: 190 us
  Pallas kernels  184 us (96%)
  local copies, waits for them, and re-layouts  4.58 us (2%)
    pallas_call x1, Pallas kernels, attention(): pl.pallas_call(attend_kernel, out_shape=(jax.ShapeDtypeStruct((4, TILE, 3...  70.4 us
    pallas_call x1, Pallas kernels, project(): pl.pallas_call(project_kernel, out_shape=(jax.ShapeDtypeStruct((3, 4, TIL...  59.5 us
    pallas_call x1, Pallas kernels, finish(): pl.pallas_call(output_kernel, out_shape=jax.ShapeDtypeStruct((6, 16, 16,...  54.4 us

profile of v1, /device:TPU:1, one launch (start us, length us, event | category | flops | bytes accessed | tf_op | source)
XLA Modules:
  0.0 190.2 jit_solution(11528516888626022024)
XLA Ops:
  0.0 1.8 copy.14
  1.8 0.0 copy-start
  1.8 59.5 %shard_map.91 = (bf16[3,4,384,128]{3,2,1,0:T(8,128)(2,1)}, bf16[3,2,2,2,384,128]{5,4,3,2,1,0:T(8,128)(2,1)}, bf16[3,2,256,128]{3,2,1,0:T(8,128)(2,1)}, bf16[4,192,384]{2,1,0:T(8,128)(2,1)}) custom-call(bf16[1536,3072]{1,0:T(8,128)(2,1)} %bitcast.5, bf16[192,1152]{1,0:T(8,128)(2,1)} %bitcast.6, bf16[192,384]{1,0:T(8,128)(2,1)} %bitcast.9, ...), custom_call_target="tpu_custom_call" | custom-call | tf_op jit(solution)/shard_map/pallas_call | solution.py:221
  61.3 0.0 copy-done
  61.3 0.7 copy.13.off
  62.7 70.4 %shard_map.92 = (bf16[4,384,384]{2,1,0:T(8,128)(2,1)}, bf16[4,2,2,192,768]{4,3,2,1,0:T(8,128)(2,1)}) custom-call(bf16[3,4,384,128]{3,2,1,0:T(8,128)(2,1)} %get-tuple-element.11.q, bf16[3,2,2,2,384,128]{5,4,3,2,1,0:T(8,128)(2,1)} %get-tuple-element.12.kv, bf16[3,2,256,128]{3,2,1,0:T(8,128)(2,1)} %get-tuple-element.13.tkv, ...), custom_call_target="tpu_custom_call" | custom-call | tf_op jit(solution)/shard_map/pallas_call | solution.py:333
  133.7 54.4 %shard_map.93 = bf16[6,16,16,192]{3,2,1,0:T(8,128)(2,1)} custom-call(bf16[4,384,384]{2,1,0:T(8,128)(2,1)} %get-tuple-element.15.att, bf16[4,2,2,192,768]{4,3,2,1,0:T(8,128)(2,1)} %get-tuple-element.16.wt, f32[1]{0:T(128)S(6)} %copy.17.guide), custom_call_target="tpu_custom_call" | custom-call | tf_op jit(solution)/shard_map/pallas_call | solution.py:416
  188.1 2.1 %copy.18 = bf16[6,16,16,192]{3,2,1,0:T(8,128)(2,1)} copy(bf16[6,16,16,192]{3,2,1,0:T(8,128)(2,1)} %shard_map.93) | data formatting | bytes 1179648
Async XLA Ops:
  1.8 59.5 %copy-start = (s32[3,2]{0,1:T(2,128)S(1)}, s32[3,2]{0,1:T(2,128)}, u32[]{:S(2)}) copy-start(s32[3,2]{0,1:T(2,128)} %param.13) | copy-start | bytes 76

commit v2 on v0

v2 whole, which is shorter than its diff:
```python
import functools
import math

import jax
import jax.numpy as jnp
from jax import lax
from jax.experimental import pallas as pl
from jax.experimental.pallas import tpu as pltpu
from jax.sharding import PartitionSpec as P

MESH = pl.DeviceIdType.MESH
BF = jnp.bfloat16
F32 = jnp.float32
VMEM = pl.BlockSpec(memory_space=pltpu.VMEM)
SMEM = pl.BlockSpec(memory_space=pltpu.SMEM)
ANY = pl.BlockSpec(memory_space=pl.ANY)
LIMIT = 62 << 20
TILE = 384
TOK = 1536


def place():
    c, t, w, h = (lax.axis_index(a) for a in ("cfg", "th", "tw", "hd"))
    return c, t, w, h // 4, lax.rem(h, 4)


def partners():
    c, t, w, x, y = place()
    return {
        "left": {"tw": lax.rem(w + 3, 4)},
        "right": {"tw": lax.rem(w + 1, 4)},
        "core": {"th": 1 - t},
        "xl": {"cfg": 1 - c},
        "xh": {"hd": (1 - x) * 4 + y},
        "xd": {"cfg": 1 - c, "hd": (1 - x) * 4 + y},
        "up": {"hd": x * 4 + lax.rem(y + 1, 4)},
        "down": {"hd": x * 4 + lax.rem(y + 3, 4)},
        "yfar": {"hd": x * 4 + lax.rem(y + 2, 4)},
    }


def greet(names):
    to = partners()
    barrier = pltpu.get_barrier_semaphore()
    for name in names:
        pl.semaphore_signal(barrier, inc=1, device_id=to[name], device_id_type=MESH)
    pl.semaphore_wait(barrier, len(names))


class Mail:
    def __init__(self, send, recv):
        self.send, self.recv, self.n, self.all = send, recv, 0, []
        self.to = partners()

    def copy(self, src, dst, name):
        k = self.n
        self.n += 1
        cp = pltpu.make_async_remote_copy(
            src_ref=src,
            dst_ref=dst,
            send_sem=self.send.at[k],
            recv_sem=self.recv.at[k],
            device_id=self.to[name],
            device_id_type=MESH,
        )
        self.all.append(cp)
        return cp

    def post(self, src, dst, name):
        cp = self.copy(src, dst, name)
        cp.start()
        return cp

    def close(self):
        for cp in self.all:
            cp.wait_send()


def normed(v, gain):
    ms = jnp.mean(v * v, axis=-1, keepdims=True)
    return v * lax.rsqrt(ms + 1e-06) * gain


SCALE = math.log2(math.e) / math.sqrt(128.0)


def weights_of(q, keys):
    s = lax.dot_general(q, keys, (((1,), (1,)), ((), ())), preferred_element_type=F32)
    return jnp.exp2(s * SCALE)


GROUP_PIECES = (((1, 0), (2, 0)), ((1, 1), (2, 1)), ((1, 2), (2, 2)), ((0, 0), (0, 1)), ((0, 2),))
N_GROUPS = len(GROUP_PIECES)
BY_Z = (0,)
N_MAIL = 192
EVERYONE = ("left", "right", "core", "xl", "xh", "xd", "up", "down", "yfar")


def sublayer_kernel(
    video, wq, wo, text, qg, kg, off, cnt, guide, out,
    xv, tv, wv0, wv1, wv2, wv3, wv4, woz, woy, wt, qb, tkv, nb0, nb1, nb2, fb0, fb1, fb2, acc_s, den_s,
    att, box, comb, cb, oacc, mid, ends, lsem, ssem, rsem,
):
    c, t, w, x, y = place()
    wv = (wv0, wv1, wv2, wv3, wv4)
    nb = (nb0, nb1, nb2)
    fb = (fb0, fb1, fb2)
    half = 768
    mine = pl.ds(2 * t, 2)
    spot = c * 2 + x
    peers = (("xd", 1 - c, 1 - x), ("xh", c, 1 - x), ("xl", 1 - c, x))

    def rows(cc, tt, ww):
        return pl.ds(pl.multiple_of((cc * 8 + tt * 4 + ww) * 192, 64), 192)

    def half_rows(cc, tt, ww, k):
        return pl.ds(pl.multiple_of((cc * 8 + tt * 4 + ww) * 192 + k * 96, 32), 96)

    own = rows(c, t, w)
    w_loads = []
    n = 4
    for g, pieces in enumerate(GROUP_PIECES):
        for k, (part, h) in enumerate(pieces):
            cp = pltpu.make_async_copy(
                wq.at[part, :, pl.ds(h * 128, 128)], wv[g].at[own, pl.ds(k * 128, 128)], lsem.at[n]
            )
            n += 1
            cp.start()
            w_loads.append(cp)
    for h in range(3):
        cp = pltpu.make_async_copy(wo.at[:, pl.ds(h * 128, 128)], woz.at[w, h], lsem.at[n])
        n += 1
        cp.start()
        w_loads.append(cp)
    loads = [
        pltpu.make_async_copy(video.at[pl.ds(i * half, half)], xv.at[pl.ds(i * half, half)], lsem.at[i])
        for i in range(2)
    ]
    loads.append(pltpu.make_async_copy(text, tv, lsem.at[2]))
    for cp in loads:
        cp.start()
    greet(EVERYONE)
    for cp in w_loads:
        cp.wait()
    mail = Mail(ssem, rsem)
    wl, wr, w2 = lax.rem(w + 3, 4), lax.rem(w + 1, 4), lax.rem(w + 2, 4)
    state = [{} for _ in range(N_GROUPS)]

    def start_own(g, names):
        for name in names:
            state[g][name] = mail.post(wv[g].at[own], wv[g].at[own], name)

    def pass_on(g, key, r, names):
        for tag, name in names:
            state[g][tag] = mail.post(wv[g].at[r], wv[g].at[r], name)

    def z_near(g):
        s = state[g]
        s["right"].wait_recv()
        pass_on(g, "r2", half_rows(c, t, wl, 0), [("r2", "right")])
        pass_on(g, "c1", rows(c, t, wl), [("c1", "core")] + ([] if g in BY_Z else [("x1", "xl")]))
        s["left"].wait_recv()
        pass_on(g, "l2", half_rows(c, t, wr, 1), [("l2", "left")])
        pass_on(g, "c2", rows(c, t, wr), [("c2", "core")] + ([] if g in BY_Z else [("x2", "xl")]))

    def z_far(g):
        s = state[g]
        s["r2"].wait_recv()
        s["l2"].wait_recv()
        pass_on(g, "x3", rows(c, t, w2), [("x3", "xl"), ("c3", "core")])

    def x_near(g):
        state[g]["xl"].wait_recv()
        names = [("d0", "core")]
        if g in BY_Z:
            names = [("x1", "right"), ("x2", "left")] + names
        pass_on(g, "d0", rows(1 - c, t, w), names)

    def x_side(g):
        state[g]["x1"].wait_recv()
        pass_on(g, "d1", rows(1 - c, t, wl), [("d1", "core")])
        state[g]["x2"].wait_recv()
        pass_on(g, "d2", rows(1 - c, t, wr), [("d2", "core")])

    def x_far(g):
        s = state[g]
        s["x3"].wait_recv()
        pass_on(g, "d3", rows(1 - c, t, w2), [("d3", "core")])
        for key in ("core", "c1", "c2", "c3", "d0", "d1", "d2", "d3"):
            s[key].wait_recv()

    def x_events(g):
        x_near(g)
        x_side(g)
        x_far(g)

    def multiply(g):
        ref, pieces = wv[g], GROUP_PIECES[g]

        def step(mc, carry):
            prod = jnp.dot(
                xv[pl.ds(pl.multiple_of(mc * half, half), half), :], ref[...], preferred_element_type=F32
            )
            for k, (part, h) in enumerate(pieces):
                v = prod[:, k * 128 : (k + 1) * 128]
                if part < 2:
                    v = normed(v, (qg if part == 0 else kg)[h : h + 1, :])
                v = v.reshape(3, 2, 8, 2, 8, 128)
                at = pl.ds(pl.multiple_of(mc * 192, 64), 192)
                for i in range(2):
                    for j in range(2):
                        tile = v[:, i, :, j].reshape(192, 128).astype(BF)
                        if part == 0:
                            qb[h, i * 2 + j, at, :] = tile
                        else:
                            nb[h][1 + j, part - 1, 2 * t + i, at, :] = tile
            return carry

        lax.fori_loop(0, 2, step, 0)
        if pieces[0][0] == 1:
            h = pieces[0][1]
            prod = jnp.dot(tv[...], ref[...], preferred_element_type=F32)
            tkv[h, 0] = normed(prod[:, :128], kg[h : h + 1, :]).astype(BF)
            tkv[h, 1] = prod[:, 128:].astype(BF)

    near, far, relays, cores = [None] * 3, [None] * 3, [[], [], []], [None] * 3

    def near_post(h):
        b = nb[h]
        near[h] = (
            (mail.post(b.at[1, :, mine], b.at[3, :, mine], "left"), b.at[3, :, mine]),
            (mail.post(b.at[2, :, mine], b.at[0, :, mine], "right"), b.at[0, :, mine]),
        )
        cores[h] = mail.post(b.at[pl.ds(1, 2), :, mine], b.at[pl.ds(1, 2), :, mine], "core")

    def far_post(h):
        b, f = nb[h], fb[h]
        far[h] = (
            (mail.post(b.at[2, :, mine], f.at[1, :, mine], "left"), f.at[1, :, mine]),
            (mail.post(b.at[1, :, mine], f.at[0, :, mine], "right"), f.at[0, :, mine]),
        )

    def relay(copies):
        passed = []
        for cp, ref in copies:
            cp.wait_recv()
            passed.append(mail.post(ref, ref, "core"))
        return passed

    def await_all(copies):
        for cp in copies:
            cp.wait_recv()

    count = cnt[0]

    def window(h, k):
        i, j = k // 2, lax.rem(k, 2)
        row = jnp.clip(2 * t + i + off[0, h], 1, 2) - 1
        col = jnp.clip(2 * w + j + off[1, h], 1, 6) + 1 - 2 * w
        return row, col, j

    def near_attend(h):
        await_all([cores[h]])

        def tile(k, carry):
            row, col, j = window(h, k)
            q = qb[h, k]
            p = weights_of(q, tkv[h, 0])
            p = jnp.where(lax.broadcasted_iota(jnp.int32, p.shape, 1) < count, p, 0.0)
            den = jnp.sum(p, axis=1, keepdims=True)
            acc = jnp.dot(p.astype(BF), tkv[h, 1], preferred_element_type=F32)
            for d in range(2):
                p = weights_of(q, nb[h][col - j + d, 0, pl.ds(row, 3)].reshape(3 * TILE, 128))
                den = den + jnp.sum(p, axis=1, keepdims=True)
                v = nb[h][col - j + d, 1, pl.ds(row, 3)].reshape(3 * TILE, 128)
                acc = acc + jnp.dot(p.astype(BF), v, preferred_element_type=F32)
            acc_s[h, k] = acc
            den_s[h, k] = jnp.broadcast_to(den, (TILE, 128))
            return carry

        lax.fori_loop(0, 4, tile, 0)

    sends = [None] * 3

    def far_tile(h, k, part=slice(0, TILE)):
        row, col, j = window(h, k)
        last = col + 2 * j
        is_far = jnp.logical_or(last == 0, last == 5)
        at = jnp.clip(last - 1, 0, 3)

        def pick(kind):
            a = fb[h][j, kind, pl.ds(row, 3)].reshape(3 * TILE, 128)
            b = nb[h][at, kind, pl.ds(row, 3)].reshape(3 * TILE, 128)
            return jnp.where(is_far, a, b)

        p = weights_of(qb[h, k, part, :], pick(0))
        den = den_s[h, k, part, :] + jnp.sum(p, axis=1, keepdims=True)
        acc = acc_s[h, k, part, :] + jnp.dot(p.astype(BF), pick(1), preferred_element_type=F32)
        return (acc / den).astype(BF)

    def far_attend(h, pieces=1):
        sends[h] = []
        for a in range(pieces):
            part = slice(a * (TILE // pieces), (a + 1) * (TILE // pieces))
            got = []
            for n, (name, cc, xx) in enumerate(peers):
                att[h, n, part, :] = far_tile(h, cc * 2 + xx, part)
                got.append(mail.post(att.at[h, n, part], box.at[h, spot, part], name))
            box[h, spot, part, :] = far_tile(h, spot, part)
            sends[h].append(got)

    y_got = [None] * 3
    gs = guide[0]
    y_lane = pl.ds(pl.multiple_of(y * 128, 128), 128)

    def mix(h, a=0, pieces=1):
        part = slice(a * (TILE // pieces), (a + 1) * (TILE // pieces))
        await_all(sends[h][a])
        for xx in range(2):
            mixed = gs * box[h, xx, part, :].astype(F32) + (1.0 - gs) * box[h, 2 + xx, part, :].astype(F32)
            comb[h, xx, part, :] = mixed.astype(BF)
        src = comb.at[h, :, part]
        y_got[h] = [mail.post(src, cb.at[h, :, part, y_lane], name) for name in ("yfar", "up", "down")]
        for xx in range(2):
            cb[h, xx, part, y_lane] = comb[h, xx, part, :]
        return y_got[h]

    def term(h, cc, xx, part=slice(0, TILE)):
        total = None
        for k in range(2):
            prod = lax.dot_general(
                cb[h, k, part, :], wt[h, k, cc, xx], (((1,), (1,)), ((), ())), preferred_element_type=F32
            )
            total = prod if total is None else total + prod
        return total

    def early_product(h):
        await_all(y_got[h])

        def dest(d, carry):
            cc, xx = d // 2, lax.rem(d, 2)
            if h == 0:
                oacc[d] = term(h, cc, xx)
            else:
                oacc[d] += term(h, cc, xx)
            return carry

        lax.fori_loop(0, 4, dest, 0)

    start_own(0, ("left", "right", "xl", "core"))
    start_own(1, ("left", "right", "xl", "core"))
    o_left = mail.post(woz.at[w], woz.at[w], "left")
    o_right = mail.post(woz.at[w], woz.at[w], "right")
    z_near(0)
    x_near(0)
    start_own(2, ("left", "right", "core"))
    z_far(0)
    z_near(1)
    x_side(0)
    start_own(2, ("xl",))
    start_own(3, ("left", "right", "core"))
    start_own(4, ("left", "right", "core"))
    z_far(1)
    o_right.wait_recv()
    o_r2 = mail.post(woz.at[wl, :, pl.ds(0, 96)], woz.at[wl, :, pl.ds(0, 96)], "right")
    o_left.wait_recv()
    o_l2 = mail.post(woz.at[wr, :, pl.ds(96, 96)], woz.at[wr, :, pl.ds(96, 96)], "left")
    z_near(2)
    z_far(2)
    start_own(3, ("xl",))
    start_own(4, ("xl",))
    x_far(0)
    for cp in loads:
        cp.wait()
    multiply(0)
    near_post(0)
    z_near(3)
    z_near(4)
    o_r2.wait_recv()
    o_l2.wait_recv()
    o_y = []
    for name, yy in (("up", lax.rem(y + 1, 4)), ("down", lax.rem(y + 3, 4)), ("yfar", lax.rem(y + 2, 4))):
        o_y.append(mail.post(woz.at[yy], woy.at[:, :, y_lane], name))
    woy[:, :, y_lane] = woz[y]
    x_events(1)
    multiply(1)
    near_post(1)
    far_post(0)
    x_events(2)
    multiply(2)
    near_post(2)
    far_post(1)
    far_post(2)
    z_far(3)
    z_far(4)
    await_all(o_y)
    o_xl = mail.post(woy, wt.at[:, x, c, t], "xl")
    o_xd = mail.post(woy, wt.at[:, x, c, t], "xd")
    o_core = [mail.post(woy, wt.at[:, x, c, t], "core")]
    o_keep = pltpu.make_async_copy(woy, wt.at[:, x, c, t], lsem.at[3])
    o_keep.start()
    relays[0] += relay(near[0])
    x_events(3)
    multiply(3)
    await_all(relays[0])
    near_attend(0)
    relays[1] += relay(near[1])
    x_events(4)
    multiply(4)
    await_all(relays[1])
    near_attend(1)
    tail = relay(far[0])
    relays[2] += relay(near[2])
    o_xl.wait_recv()
    at = wt.at[:, x, 1 - c, t]
    o_core.append(mail.post(at, at, "core"))
    o_xf = mail.post(at, at, "xd")
    o_xd.wait_recv()
    at = wt.at[:, 1 - x, 1 - c, t]
    o_core.append(mail.post(at, at, "core"))
    await_all(tail)
    far_attend(0)
    await_all(relays[2])
    near_attend(2)
    mix(0)
    tail = relay(far[1])
    await_all(tail)
    far_attend(1)
    o_xf.wait_recv()
    at = wt.at[:, 1 - x, c, t]
    o_core.append(mail.post(at, at, "core"))
    mix(1)
    o_keep.wait()
    await_all(o_core)
    early_product(0)
    tail = relay(far[2])
    await_all(tail)
    far_attend(2, 2)
    early_product(1)
    y_half = [mix(2, 0, 2), mix(2, 1, 2)]
    last = []
    for a in range(2):
        part = slice(a * 192, (a + 1) * 192)
        await_all(y_half[a])
        for n, (name, cc, xx) in enumerate(peers):
            mid[n, part, :] = (oacc[cc * 2 + xx, part, :] + term(2, cc, xx, part)).astype(BF)
            last.append(mail.post(mid.at[n, part], ends.at[spot, part], name))
        ends[spot, part, :] = (oacc[spot, part, :] + term(2, c, x, part)).astype(BF)
    await_all(last)
    for i in range(2):
        sides = [ends[i * 2 + j].astype(F32).reshape(6, 8, 8, 192) for j in range(2)]
        out[:, i * 8 : (i + 1) * 8] = jnp.concatenate(sides, axis=2).astype(BF)
    mail.close()


def sublayer(video, wq, wo, text, qg, kg, off, cnt, guide):
    near = pltpu.VMEM((4, 2, 4, TILE, 128), BF)
    far = pltpu.VMEM((2, 2, 4, TILE, 128), BF)
    return pl.pallas_call(
        sublayer_kernel,
        out_shape=jax.ShapeDtypeStruct((6, 16, 16, 192), BF),
        in_specs=[ANY, ANY, ANY, ANY, VMEM, VMEM, SMEM, SMEM, SMEM],
        out_specs=VMEM,
        scratch_shapes=[
            pltpu.VMEM((TOK, 3072), BF),
            pltpu.VMEM((256, 3072), BF),
            pltpu.VMEM((3072, 256), BF),
            pltpu.VMEM((3072, 256), BF),
            pltpu.VMEM((3072, 256), BF),
            pltpu.VMEM((3072, 256), BF),
            pltpu.VMEM((3072, 128), BF),
            pltpu.VMEM((4, 3, 192, 128), BF),
            pltpu.VMEM((3, 192, 512), BF),
            pltpu.VMEM((3, 2, 2, 2, 192, 512), BF),
            pltpu.VMEM((3, 4, TILE, 128), BF),
            pltpu.VMEM((3, 2, 256, 128), BF),
            near,
            near,
            near,
            far,
            far,
            far,
            pltpu.VMEM((3, 4, TILE, 128), F32),
            pltpu.VMEM((3, 4, TILE, 128), F32),
            pltpu.VMEM((3, 3, TILE, 128), BF),
            pltpu.VMEM((3, 4, TILE, 128), BF),
            pltpu.VMEM((3, 2, TILE, 128), BF),
            pltpu.VMEM((3, 2, TILE, 512), BF),
            pltpu.VMEM((4, TILE, 192), F32),
            pltpu.VMEM((3, TILE, 192), BF),
            pltpu.VMEM((4, TILE, 192), BF),
            pltpu.SemaphoreType.DMA((20,)),
            pltpu.SemaphoreType.DMA((N_MAIL,)),
            pltpu.SemaphoreType.DMA((N_MAIL,)),
        ],
        compiler_params=pltpu.CompilerParams(collective_id=0, has_side_effects=True, vmem_limit_bytes=LIMIT),
    )(video, wq, wo, text, qg, kg, off, cnt, guide)


def body(video, text_states, text_count, guidance, window_offsets, w_qkv, q_gain, k_gain, w_out):
    return sublayer(
        video.reshape(TOK, 3072),
        w_qkv.swapaxes(0, 1),
        w_out.T,
        text_states[0],
        q_gain,
        k_gain,
        window_offsets.T,
        text_count,
        guidance,
    )


def solution(mesh):
    return jax.shard_map(
        body,
        mesh=mesh,
        in_specs=(
            P("cfg", None, "th", "tw", None),
            P("cfg", None, None),
            P("cfg"),
            P(),
            P("hd", None),
            P(("cfg", "th", "tw"), None, "hd"),
            P("hd", None),
            P("hd", None),
            P("hd", ("cfg", "th", "tw")),
        ),
        out_specs=P(None, "th", "tw", ("cfg", "hd")),
        check_vma=False,
    )
```

time: 698 us -> 138 us (0.20)
  waiting for transfers between devices: 425 us -> 0 us
  Pallas kernels: 0 us -> 133 us
  local copies, waits for them, and re-layouts: 98.8 us -> 2.1 us
  matrix products: 68.4 us -> 0 us
  loops' own time: 42.6 us -> 0 us
  other arithmetic: 35.4 us -> 0 us
  between operations: 14 us -> 1.31 us
  starting transfers between devices: 11.9 us -> 0 us
    reduce_scatter x1 -> x0, waiting for transfers between devices: 211 us -> none  [body(): lax.psum_scatter(partial_terms, ('cfg', 'hd'), scatter_dimension=1, tiled...]
    ppermute x4 -> x0, waiting for transfers between devices: 154 us -> none  [the longest x2 151 us: extended(): lax.ppermute(head, axis, [((i + 1) % count, i) for i in range(ends)])]
    pallas_call x0 -> x1, Pallas kernels: none -> 133 us  [sublayer(): pl.pallas_call(sublayer_kernel, out_shape=jax.ShapeDtypeStruct((6, 16, 16...]
    dot_general x51 -> x0, matrix products: 68.4 us -> none  [the longest x1 16 us: body(): jnp.dot(flat_rows, weight_piece.reshape(span, 3 * group_width), preferred...]
    all_gather x2 -> x0, waiting for transfers between devices: 59.2 us -> none  [the longest x1 59.2 us: body(): lax.all_gather(w_qkv, ('cfg', 'th', 'tw'), axis=0, tiled=True)]
    another operation x1 -> x0, loops' own time: 42.6 us -> none  [body(): lax.map(pair_output, jnp.arange(head_local * tiles_down * tiles_across, d...]
    dynamic_slice x48 -> x0, local copies, waits for them, and re-layouts: 40.2 us -> none  [the longest x12 21.7 us: pair_output(): lax.dynamic_slice(padded, (zero, rim_row, rim_col, head * head_size), (n_...]
    slice x16 -> x0, local copies, waits for them, and re-layouts: 28.2 us -> none  [the longest x2 8.44 us: body(): values = proj[:, 2].astype(jnp.bfloat16)]
  transfers between devices with their start and end apart: 7 -> 0, of which waited for: 6 -> 0; matrix products, arithmetic and copies ran while one was open for 17% -> 0% of each run, Pallas kernels for 0% -> 0%
where the time goes in v2:
time: 138 us; the launch traced here: 137 us
  Pallas kernels  133 us (96%)
  local copies, waits for them, and re-layouts  2.1 us (2%)
    pallas_call x1, Pallas kernels, sublayer(): pl.pallas_call(sublayer_kernel, out_shape=jax.ShapeDtypeStruct((6, 16, 16...  133 us

profile of v2, /device:TPU:1, one launch (start us, length us, event | category | flops | bytes accessed | tf_op | source)
XLA Modules:
  0.0 136.9 jit_solution(16444262670012504947)
XLA Ops:
  1.3 133.5 %shard_map.91 = bf16[6,16,16,192]{3,2,1,0:T(8,128)(2,1)} custom-call(bf16[1536,3072]{1,0:T(8,128)(2,1)} %bitcast.5, bf16[3,192,384]{2,1,0:T(8,128)(2,1)} %bitcast.7, bf16[192,384]{1,0:T(8,128)(2,1)} %bitcast.8, bf16[256,3072]{1,0:T(8,128)(2,1)} %bitcast.6, f32[3,128]{1,0:T(4,128)} %qg.1, f32[3,128]{1,0:T(4,128)} %kg.1, s32[2,3]{1,0:T(2,128)} %bitcast.9, ...), custom_call_target="tpu_custom_call" | custom-call | tf_op jit(solution)/shard_map/pallas_call | solution.py:459
  134.8 2.1 %copy.13 = bf16[6,16,16,192]{3,2,1,0:T(8,128)(2,1)} copy(bf16[6,16,16,192]{3,2,1,0:T(8,128)(2,1)} %shard_map.91) | data formatting | bytes 1179648

commit v3 on v2

--- a/solution.py
+++ b/solution.py
@@ -89,10 +89,12 @@
     return jnp.exp2(s * SCALE)
 
 
-GROUP_PIECES = (((1, 0), (2, 0)), ((1, 1), (2, 1)), ((1, 2), (2, 2)), ((0, 0), (0, 1)), ((0, 2),))
+GROUP_PIECES = (((1, 0), (2, 0)), ((0, 0), (0, 1)), ((1, 1), (2, 1)), ((1, 2), (2, 2)), ((0, 2),))
 N_GROUPS = len(GROUP_PIECES)
 BY_Z = (0,)
-N_MAIL = 192
+FRAMES = 3
+PIECES = 2
+N_MAIL = 224
 EVERYONE = ("left", "right", "core", "xl", "xh", "xd", "up", "down", "yfar")
 
 
@@ -197,6 +199,9 @@
     def multiply(g):
         ref, pieces = wv[g], GROUP_PIECES[g]
 
+        frames = FRAMES
+        half = 256 * frames
+
         def step(mc, carry):
             prod = jnp.dot(
                 xv[pl.ds(pl.multiple_of(mc * half, half), half), :], ref[...], preferred_element_type=F32
@@ -205,18 +210,18 @@
                 v = prod[:, k * 128 : (k + 1) * 128]
                 if part < 2:
                     v = normed(v, (qg if part == 0 else kg)[h : h + 1, :])
-                v = v.reshape(3, 2, 8, 2, 8, 128)
-                at = pl.ds(pl.multiple_of(mc * 192, 64), 192)
+                v = v.reshape(frames, 2, 8, 2, 8, 128)
+                at = pl.ds(pl.multiple_of(mc * 64 * frames, 64), 64 * frames)
                 for i in range(2):
                     for j in range(2):
-                        tile = v[:, i, :, j].reshape(192, 128).astype(BF)
+                        tile = v[:, i, :, j].reshape(64 * frames, 128).astype(BF)
                         if part == 0:
                             qb[h, i * 2 + j, at, :] = tile
                         else:
                             nb[h][1 + j, part - 1, 2 * t + i, at, :] = tile
             return carry
 
-        lax.fori_loop(0, 2, step, 0)
+        lax.fori_loop(0, 6 // frames, step, 0)
         if pieces[0][0] == 1:
             h = pieces[0][1]
             prod = jnp.dot(tv[...], ref[...], preferred_element_type=F32)
@@ -298,16 +303,14 @@
         acc = acc_s[h, k, part, :] + jnp.dot(p.astype(BF), pick(1), preferred_element_type=F32)
         return (acc / den).astype(BF)
 
-    def far_attend(h, pieces=1):
-        sends[h] = []
-        for a in range(pieces):
-            part = slice(a * (TILE // pieces), (a + 1) * (TILE // pieces))
-            got = []
-            for n, (name, cc, xx) in enumerate(peers):
-                att[h, n, part, :] = far_tile(h, cc * 2 + xx, part)
-                got.append(mail.post(att.at[h, n, part], box.at[h, spot, part], name))
-            box[h, spot, part, :] = far_tile(h, spot, part)
-            sends[h].append(got)
+    def far_attend(h):
+        def tile(k, carry):
+            att[h, k] = far_tile(h, k)
+            return carry
+
+        lax.fori_loop(0, 4, tile, 0)
+        sends[h] = [mail.post(att.at[h, cc * 2 + xx], box.at[h, spot], name) for name, cc, xx in peers]
+        box[h, spot] = att[h, spot]
 
     y_got = [None] * 3
     gs = guide[0]
@@ -315,7 +318,8 @@
 
     def mix(h, a=0, pieces=1):
         part = slice(a * (TILE // pieces), (a + 1) * (TILE // pieces))
-        await_all(sends[h][a])
+        if a == 0:
+            await_all(sends[h])
         for xx in range(2):
             mixed = gs * box[h, xx, part, :].astype(F32) + (1.0 - gs) * box[h, 2 + xx, part, :].astype(F32)
             comb[h, xx, part, :] = mixed.astype(BF)
@@ -353,11 +357,10 @@
     o_right = mail.post(woz.at[w], woz.at[w], "right")
     z_near(0)
     x_near(0)
-    start_own(2, ("left", "right", "core"))
+    start_own(2, ("left", "right", "core", "xl"))
     z_far(0)
     z_near(1)
     x_side(0)
-    start_own(2, ("xl",))
     start_own(3, ("left", "right", "core"))
     start_own(4, ("left", "right", "core"))
     z_far(1)
@@ -368,14 +371,17 @@
     z_near(2)
     z_far(2)
     start_own(3, ("xl",))
+    x_far(0)
+    z_near(3)
     start_own(4, ("xl",))
-    x_far(0)
+    z_near(4)
     for cp in loads:
         cp.wait()
     multiply(0)
     near_post(0)
-    z_near(3)
-    z_near(4)
+    far_post(0)
+    z_far(3)
+    z_far(4)
     o_r2.wait_recv()
     o_l2.wait_recv()
     o_y = []
@@ -384,64 +390,75 @@
     woy[:, :, y_lane] = woz[y]
     x_events(1)
     multiply(1)
-    near_post(1)
-    far_post(0)
     x_events(2)
     multiply(2)
-    near_post(2)
+    near_post(1)
     far_post(1)
-    far_post(2)
-    z_far(3)
-    z_far(4)
     await_all(o_y)
-    o_xl = mail.post(woy, wt.at[:, x, c, t], "xl")
-    o_xd = mail.post(woy, wt.at[:, x, c, t], "xd")
-    o_core = [mail.post(woy, wt.at[:, x, c, t], "core")]
+    o_xl, o_xd, o_xf, o_core = [None] * 3, [None] * 3, [None] * 3, [[], [], []]
+    for h in range(3):
+        o_xl[h] = mail.post(woy.at[h], wt.at[h, x, c, t], "xl")
+        o_xd[h] = mail.post(woy.at[h], wt.at[h, x, c, t], "xd")
+        o_core[h].append(mail.post(woy.at[h], wt.at[h, x, c, t], "core"))
+
+    def o_cross(h):
+        o_xl[h].wait_recv()
+        at = wt.at[h, x, 1 - c, t]
+        o_core[h].append(mail.post(at, at, "core"))
+        o_xf[h] = mail.post(at, at, "xd")
+        o_xd[h].wait_recv()
+        at = wt.at[h, 1 - x, 1 - c, t]
+        o_core[h].append(mail.post(at, at, "core"))
+
+    def o_last(h):
+        o_xf[h].wait_recv()
+        at = wt.at[h, 1 - x, c, t]
+        o_core[h].append(mail.post(at, at, "core"))
+
     o_keep = pltpu.make_async_copy(woy, wt.at[:, x, c, t], lsem.at[3])
     o_keep.start()
     relays[0] += relay(near[0])
+    await_all(relays[0])
+    near_attend(0)
     x_events(3)
     multiply(3)
-    await_all(relays[0])
-    near_attend(0)
-    relays[1] += relay(near[1])
+    near_post(2)
+    far_post(2)
+    tail = relay(far[0])
+    await_all(tail)
+    far_attend(0)
     x_events(4)
     multiply(4)
+    relays[1] += relay(near[1])
     await_all(relays[1])
+    o_cross(0)
     near_attend(1)
-    tail = relay(far[0])
+    tail = relay(far[1])
+    mix(0)
+    o_cross(1)
+    await_all(tail)
+    far_attend(1)
+    o_cross(2)
     relays[2] += relay(near[2])
-    o_xl.wait_recv()
-    at = wt.at[:, x, 1 - c, t]
-    o_core.append(mail.post(at, at, "core"))
-    o_xf = mail.post(at, at, "xd")
-    o_xd.wait_recv()
-    at = wt.at[:, 1 - x, 1 - c, t]
-    o_core.append(mail.post(at, at, "core"))
-    await_all(tail)
-    far_attend(0)
     await_all(relays[2])
     near_attend(2)
-    mix(0)
-    tail = relay(far[1])
-    await_all(tail)
-    far_attend(1)
-    o_xf.wait_recv()
-    at = wt.at[:, 1 - x, c, t]
-    o_core.append(mail.post(at, at, "core"))
     mix(1)
-    o_keep.wait()
-    await_all(o_core)
-    early_product(0)
     tail = relay(far[2])
     await_all(tail)
-    far_attend(2, 2)
+    far_attend(2)
+    o_keep.wait()
+    for h in range(3):
+        o_last(h)
+    await_all(o_core[0])
+    early_product(0)
+    await_all(o_core[1])
     early_product(1)
-    y_half = [mix(2, 0, 2), mix(2, 1, 2)]
+    await_all(o_core[2])
+    y_parts = [mix(2, a, PIECES) for a in range(PIECES)]
     last = []
-    for a in range(2):
-        part = slice(a * 192, (a + 1) * 192)
-        await_all(y_half[a])
+    for a in range(PIECES):
+        part = slice(a * (TILE // PIECES), (a + 1) * (TILE // PIECES))
+        await_all(y_parts[a])
         for n, (name, cc, xx) in enumerate(peers):
             mid[n, part, :] = (oacc[cc * 2 + xx, part, :] + term(2, cc, xx, part)).astype(BF)
             last.append(mail.post(mid.at[n, part], ends.at[spot, part], name))
@@ -482,7 +499,7 @@
             far,
             pltpu.VMEM((3, 4, TILE, 128), F32),
             pltpu.VMEM((3, 4, TILE, 128), F32),
-            pltpu.VMEM((3, 3, TILE, 128), BF),
+            pltpu.VMEM((3, 4, TILE, 128), BF),
             pltpu.VMEM((3, 4, TILE, 128), BF),
             pltpu.VMEM((3, 2, TILE, 128), BF),
             pltpu.VMEM((3, 2, TILE, 512), BF),

time: 138 us -> 129 us (0.935)
  Pallas kernels: 133 us -> 126 us
    pallas_call x1, Pallas kernels: 133 us -> 126 us  [sublayer(): pl.pallas_call(sublayer_kernel, out_shape=jax.ShapeDtypeStruct((6, 16, 16...]
where the time goes in v3:
time: 129 us
  Pallas kernels  126 us (98%)
  local copies, waits for them, and re-layouts  2.1 us (2%)
  between operations  1.31 us (1%)
    pallas_call x1, Pallas kernels, sublayer(): pl.pallas_call(sublayer_kernel, out_shape=jax.ShapeDtypeStruct((6, 16, 16...  126 us

profile of v3, /device:TPU:1, one launch (start us, length us, event | category | flops | bytes accessed | tf_op | source)
XLA Modules:
  0.0 128.9 jit_solution(6221707957697799189)
XLA Ops:
  1.3 125.5 %shard_map.91 = bf16[6,16,16,192]{3,2,1,0:T(8,128)(2,1)} custom-call(bf16[1536,3072]{1,0:T(8,128)(2,1)} %bitcast.5, bf16[3,192,384]{2,1,0:T(8,128)(2,1)} %bitcast.7, bf16[192,384]{1,0:T(8,128)(2,1)} %bitcast.8, bf16[256,3072]{1,0:T(8,128)(2,1)} %bitcast.6, f32[3,128]{1,0:T(4,128)} %qg.1, f32[3,128]{1,0:T(4,128)} %kg.1, s32[2,3]{1,0:T(2,128)} %bitcast.9, ...), custom_call_target="tpu_custom_call" | custom-call | tf_op jit(solution)/shard_map/pallas_call | solution.py:476
  126.8 2.1 %copy.13 = bf16[6,16,16,192]{3,2,1,0:T(8,128)(2,1)} copy(bf16[6,16,16,192]{3,2,1,0:T(8,128)(2,1)} %shard_map.91) | data formatting | bytes 1179648

commit v4 on v3

--- a/solution.py
+++ b/solution.py
@@ -89,11 +89,11 @@
     return jnp.exp2(s * SCALE)
 
 
-GROUP_PIECES = (((1, 0), (2, 0)), ((0, 0), (0, 1)), ((1, 1), (2, 1)), ((1, 2), (2, 2)), ((0, 2),))
+GROUP_PIECES = (((1, 0), (2, 0)), ((1, 1), (2, 1)), ((0, 0), (0, 1)), ((1, 2), (2, 2)), ((0, 2),))
 N_GROUPS = len(GROUP_PIECES)
 BY_Z = (0,)
 FRAMES = 3
-PIECES = 2
+PIECES = 4
 N_MAIL = 224
 EVERYONE = ("left", "right", "core", "xl", "xh", "xd", "up", "down", "yfar")
 
@@ -222,11 +222,11 @@
             return carry
 
         lax.fori_loop(0, 6 // frames, step, 0)
-        if pieces[0][0] == 1:
-            h = pieces[0][1]
-            prod = jnp.dot(tv[...], ref[...], preferred_element_type=F32)
-            tkv[h, 0] = normed(prod[:, :128], kg[h : h + 1, :]).astype(BF)
-            tkv[h, 1] = prod[:, 128:].astype(BF)
+    def text_product(g):
+        ref, h = wv[g], GROUP_PIECES[g][0][1]
+        prod = jnp.dot(tv[...], ref[...], preferred_element_type=F32)
+        tkv[h, 0] = normed(prod[:, :128], kg[h : h + 1, :]).astype(BF)
+        tkv[h, 1] = prod[:, 128:].astype(BF)
 
     near, far, relays, cores = [None] * 3, [None] * 3, [[], [], []], [None] * 3
 
@@ -303,13 +303,18 @@
         acc = acc_s[h, k, part, :] + jnp.dot(p.astype(BF), pick(1), preferred_element_type=F32)
         return (acc / den).astype(BF)
 
-    def far_attend(h):
-        def tile(k, carry):
-            att[h, k] = far_tile(h, k)
+    def far_attend(h, runs=1):
+        def tile(n, carry):
+            cc = c + (1 - 2 * c) * (1 - lax.rem(n, 2))
+            xx = x + (1 - 2 * x) * (1 - n // 2)
+            att[h, cc * 2 + xx] = far_tile(h, cc * 2 + xx)
             return carry
 
-        lax.fori_loop(0, 4, tile, 0)
-        sends[h] = [mail.post(att.at[h, cc * 2 + xx], box.at[h, spot], name) for name, cc, xx in peers]
+        sends[h] = []
+        for n in range(runs):
+            lax.fori_loop(n * 4 // runs, (n + 1) * 4 // runs, tile, 0)
+            for name, cc, xx in peers[n * 4 // runs : (n + 1) * 4 // runs]:
+                sends[h].append(mail.post(att.at[h, cc * 2 + xx], box.at[h, spot], name))
         box[h, spot] = att[h, spot]
 
     y_got = [None] * 3
@@ -382,6 +387,7 @@
     far_post(0)
     z_far(3)
     z_far(4)
+    text_product(0)
     o_r2.wait_recv()
     o_l2.wait_recv()
     o_y = []
@@ -390,10 +396,11 @@
     woy[:, :, y_lane] = woz[y]
     x_events(1)
     multiply(1)
+    near_post(1)
+    far_post(1)
+    text_product(1)
     x_events(2)
     multiply(2)
-    near_post(1)
-    far_post(1)
     await_all(o_y)
     o_xl, o_xd, o_xf, o_core = [None] * 3, [None] * 3, [None] * 3, [[], [], []]
     for h in range(3):
@@ -418,12 +425,13 @@
     o_keep = pltpu.make_async_copy(woy, wt.at[:, x, c, t], lsem.at[3])
     o_keep.start()
     relays[0] += relay(near[0])
-    await_all(relays[0])
-    near_attend(0)
     x_events(3)
     multiply(3)
     near_post(2)
     far_post(2)
+    text_product(3)
+    await_all(relays[0])
+    near_attend(0)
     tail = relay(far[0])
     await_all(tail)
     far_attend(0)
@@ -445,7 +453,7 @@
     mix(1)
     tail = relay(far[2])
     await_all(tail)
-    far_attend(2)
+    far_attend(2, 2)
     o_keep.wait()
     for h in range(3):
         o_last(h)

time: 129 us -> 125 us (0.969)
  Pallas kernels: 126 us -> 121 us
    pallas_call x1, Pallas kernels: 126 us -> 121 us  [sublayer(): pl.pallas_call(sublayer_kernel, out_shape=jax.ShapeDtypeStruct((6, 16, 16...]
where the time goes in v4:
time: 125 us; the launch traced here: 124 us
  Pallas kernels  121 us (97%)
  local copies, waits for them, and re-layouts  2.1 us (2%)
  between operations  1.31 us (1%)
    pallas_call x1, Pallas kernels, sublayer(): pl.pallas_call(sublayer_kernel, out_shape=jax.ShapeDtypeStruct((6, 16, 16...  121 us

profile of v4, /device:TPU:1, one launch (start us, length us, event | category | flops | bytes accessed | tf_op | source)
XLA Modules:
  0.0 124.4 jit_solution(13318654665476305676)
XLA Ops:
  1.3 121.0 %shard_map.91 = bf16[6,16,16,192]{3,2,1,0:T(8,128)(2,1)} custom-call(bf16[1536,3072]{1,0:T(8,128)(2,1)} %bitcast.5, bf16[3,192,384]{2,1,0:T(8,128)(2,1)} %bitcast.7, bf16[192,384]{1,0:T(8,128)(2,1)} %bitcast.8, bf16[256,3072]{1,0:T(8,128)(2,1)} %bitcast.6, f32[3,128]{1,0:T(4,128)} %qg.1, f32[3,128]{1,0:T(4,128)} %kg.1, s32[2,3]{1,0:T(2,128)} %bitcast.9, ...), custom_call_target="tpu_custom_call" | custom-call | tf_op jit(solution)/shard_map/pallas_call | solution.py:484
  122.3 2.1 %copy.13 = bf16[6,16,16,192]{3,2,1,0:T(8,128)(2,1)} copy(bf16[6,16,16,192]{3,2,1,0:T(8,128)(2,1)} %shard_map.91) | data formatting | bytes 1179648

commit v5 on v4

--- a/solution.py
+++ b/solution.py
@@ -329,7 +329,7 @@
             mixed = gs * box[h, xx, part, :].astype(F32) + (1.0 - gs) * box[h, 2 + xx, part, :].astype(F32)
             comb[h, xx, part, :] = mixed.astype(BF)
         src = comb.at[h, :, part]
-        y_got[h] = [mail.post(src, cb.at[h, :, part, y_lane], name) for name in ("yfar", "up", "down")]
+        y_got[h] = [mail.post(src, cb.at[h, :, part, y_lane], name) for name in ("up", "down", "yfar")]
         for xx in range(2):
             cb[h, xx, part, y_lane] = comb[h, xx, part, :]
         return y_got[h]
@@ -432,11 +432,11 @@
     text_product(3)
     await_all(relays[0])
     near_attend(0)
+    x_events(4)
+    multiply(4)
     tail = relay(far[0])
     await_all(tail)
     far_attend(0)
-    x_events(4)
-    multiply(4)
     relays[1] += relay(near[1])
     await_all(relays[1])
     o_cross(0)
@@ -459,10 +459,10 @@
         o_last(h)
     await_all(o_core[0])
     early_product(0)
+    y_parts = [mix(2, a, PIECES) for a in range(PIECES)]
     await_all(o_core[1])
     early_product(1)
     await_all(o_core[2])
-    y_parts = [mix(2, a, PIECES) for a in range(PIECES)]
     last = []
     for a in range(PIECES):
         part = slice(a * (TILE // PIECES), (a + 1) * (TILE // PIECES))

time: 125 us -> 121 us (0.968)
  Pallas kernels: 121 us -> 117 us
    pallas_call x1, Pallas kernels: 121 us -> 117 us  [sublayer(): pl.pallas_call(sublayer_kernel, out_shape=jax.ShapeDtypeStruct((6, 16, 16...]
where the time goes in v5:
time: 121 us
  Pallas kernels  117 us (97%)
  local copies, waits for them, and re-layouts  2.1 us (2%)
  between operations  1.31 us (1%)
    pallas_call x1, Pallas kernels, sublayer(): pl.pallas_call(sublayer_kernel, out_shape=jax.ShapeDtypeStruct((6, 16, 16...  117 us

profile of v5, /device:TPU:1, one launch (start us, length us, event | category | flops | bytes accessed | tf_op | source)
XLA Modules:
  0.0 120.6 jit_solution(11411627243995880280)
XLA Ops:
  1.3 117.2 %shard_map.91 = bf16[6,16,16,192]{3,2,1,0:T(8,128)(2,1)} custom-call(bf16[1536,3072]{1,0:T(8,128)(2,1)} %bitcast.5, bf16[3,192,384]{2,1,0:T(8,128)(2,1)} %bitcast.7, bf16[192,384]{1,0:T(8,128)(2,1)} %bitcast.8, bf16[256,3072]{1,0:T(8,128)(2,1)} %bitcast.6, f32[3,128]{1,0:T(4,128)} %qg.1, f32[3,128]{1,0:T(4,128)} %kg.1, s32[2,3]{1,0:T(2,128)} %bitcast.9, ...), custom_call_target="tpu_custom_call" | custom-call | tf_op jit(solution)/shard_map/pallas_call | solution.py:484
  118.5 2.1 %copy.13 = bf16[6,16,16,192]{3,2,1,0:T(8,128)(2,1)} copy(bf16[6,16,16,192]{3,2,1,0:T(8,128)(2,1)} %shard_map.91) | data formatting | bytes 1179648
